TPU v7x, 32 devices: a whole 2x2x4 slice. The times are simulated.
32 devices in a mesh: dp: 8 (over z, x), tensor: 4 (over y, core).
Axes of the slice: x: 2, y: 2, z: 4, core: 2. Of those that a mesh axis runs over, the one named last changes fastest.
Arguments:
- tokens_in: bfloat16 [12288, 768], P('dp'), may hold values from -6 to 6
- cotangent: bfloat16 [12288, 768], P('dp'), may hold values from -6 to 6
- span_mask: int32 [12288], P('dp'), may hold values from 0 to 1, as said below
- lengths: int32 [24], P('dp'), may hold values from 128 to 512, as said below
- step: int32 [1], replicated, may hold values from 1000 to 31999
- warmup: int32 [1], replicated, may hold values from 1000 to 29999
- total: int32 [1], replicated, may hold values from 32000 to 40000
- w_qkv: float32 [768, 3, 768], P(None, None, 'tensor'), may hold values from -0.21875 to 0.21875
- w_out: float32 [768, 768], P(None, 'tensor'), may hold values from -1.25 to 1.25
- w_in: float32 [768, 3072], P(None, 'tensor'), may hold values from -0.21875 to 0.21875
- w_back: float32 [768, 3072], P(None, 'tensor'), may hold values from -0.109375 to 0.109375
- gains: float32 [2, 768], replicated, may hold values from 0.5 to 1.5
- biases: float32 [6, 768], replicated, may hold values from -3 to 3
- bias_in: float32 [3072], replicated, may hold values from -3 to 3
- mom_qkv: float32 [2, 768, 3, 768], P(None, 'dp', None, 'tensor'), as said below
- mom_out: float32 [2, 768, 768], P(None, 'dp', 'tensor'), as said below
- mom_in: float32 [2, 768, 3072], P(None, 'dp', 'tensor'), as said below
- mom_back: float32 [2, 768, 3072], P(None, 'dp', 'tensor'), as said below
- mom_gains: float32 [2, 2, 768], replicated, as said below
- mom_biases: float32 [2, 6, 768], replicated, as said below
- mom_bias_in: float32 [2, 3072], replicated, as said below
Outputs:
- normed_out: bfloat16 [12288, 768], P('dp')
- input_grad: float32 [12288, 768], P('dp')
- change_qkv: float32 [768, 3, 768], P(None, None, 'tensor')
- change_out_proj: float32 [768, 768], P(None, 'tensor')
- change_in_proj: float32 [768, 3072], P(None, 'tensor')
- change_back_proj: float32 [768, 3072], P(None, 'tensor')
- change_gains: float32 [2, 768], replicated
- change_biases: float32 [6, 768], replicated
- change_bias_in: float32 [3072], replicated
- new_mom_qkv: float32 [2, 768, 3, 768], P(None, 'dp', None, 'tensor')
- new_mom_out: float32 [2, 768, 768], P(None, 'dp', 'tensor')
- new_mom_in: float32 [2, 768, 3072], P(None, 'dp', 'tensor')
- new_mom_back: float32 [2, 768, 3072], P(None, 'dp', 'tensor')
- new_mom_gains: float32 [2, 2, 768], replicated
- new_mom_biases: float32 [2, 6, 768], replicated
- new_mom_bias_in: float32 [2, 3072], replicated
Inputs may be any that keep to these rules, and one draw needn't show every extreme that they name: `span_mask`: marked positions lie below their sequence's length and form unions of spans of 1 to 10 positions; each sequence has at most 76 of them, and in every draw each of the 3 sequences of some index of dp has exactly 76. `lengths`: a sequence's real tokens stand at its start, the rest is padding. step < total. warmup < total. `mom_qkv`: index 1 of the leading dimension holds positive second moments. `mom_out`: index 1 of the leading dimension holds positive second moments. `mom_in`: index 1 of the leading dimension holds positive second moments. `mom_back`: index 1 of the leading dimension holds positive second moments. `mom_gains`: index 1 of the leading dimension holds positive second moments. `mom_biases`: index 1 of the leading dimension holds positive second moments. `mom_bias_in`: index 1 of the leading dimension holds positive second moments.
All inputs are finite; a program needn't handle non-finite values.
Results may differ from a plain program's by a relative error of at most 0.017.
The roundings to bfloat16 on the way count: a program that leaves them out, or rounds other values in their place, can miss the bound.
Values sent between devices are 32-bit elements; how exact they have to be, the bound alone decides.
A program may use at most 128 MiB of HBM per device.

v0:
```python
import math
import jax
import jax.numpy as jnp
from jax import lax
from jax.sharding import PartitionSpec as P

HD = 64
SPAN_ROWS = 80
NORM_EPS = 1e-12
BETA_ONE = 0.9
BETA_TWO = 0.999
ADAM_EPS = 1e-06
WEIGHT_DECAY = 0.01


def layer_norm(values, gain, shift):
    center = values - jnp.mean(values, axis=-1, keepdims=True)
    spread = jnp.mean(center * center, axis=-1, keepdims=True)
    return center * lax.rsqrt(spread + NORM_EPS) * gain + shift


def exact_gelu(values):
    return jax.nn.gelu(values, approximate=False)


def outer_sum(left, right):
    return jnp.einsum("ta,tb->ab", left, right, preferred_element_type=jnp.float32)


def adam_step(weight, grad, moments, ratio, corr_one, corr_two, decay):
    first = BETA_ONE * moments[0] + (1.0 - BETA_ONE) * grad
    second = BETA_TWO * moments[1] + (1.0 - BETA_TWO) * grad * grad
    update = first / corr_one / (jnp.sqrt(second / corr_two) + ADAM_EPS) + decay * weight
    return (-ratio * update, jnp.stack([first, second]))


def on_device(
    tokens_in,
    cotangent,
    span_mask,
    lengths,
    step,
    warmup,
    total,
    w_qkv,
    w_out,
    w_in,
    w_back,
    gains,
    biases,
    bias_in,
    mom_qkv,
    mom_out,
    mom_in,
    mom_back,
    mom_gains,
    mom_biases,
    mom_bias_in,
):
    row_count, model_width = tokens_in.shape
    seq_count = lengths.shape[0]
    seq_length = row_count // seq_count
    head_cols = w_qkv.shape[2]
    hidden_cols = w_in.shape[1]
    head_size = HD
    local_heads = head_cols // head_size
    query_scale = 1.0 / math.sqrt(head_size)
    tensor_slot = lax.axis_index("tensor")
    bias_query = lax.dynamic_slice_in_dim(biases[0], tensor_slot * head_cols, head_cols)
    bias_value = lax.dynamic_slice_in_dim(biases[1], tensor_slot * head_cols, head_cols)
    bias_hidden = lax.dynamic_slice_in_dim(bias_in, tensor_slot * hidden_cols, hidden_cols)
    qkv_low = w_qkv.astype(jnp.bfloat16).reshape(model_width, 3 * head_cols)
    out_low = w_out.astype(jnp.bfloat16)
    in_low = w_in.astype(jnp.bfloat16)
    down_low = w_back.astype(jnp.bfloat16)
    projected = jnp.dot(tokens_in, qkv_low, preferred_element_type=jnp.float32).reshape(
        row_count, 3, head_cols
    )
    attn_shape = (seq_count, seq_length, local_heads, head_size)
    queries = (
        ((projected[:, 0] + bias_query) * query_scale).astype(jnp.bfloat16).reshape(attn_shape)
    )
    keys = projected[:, 1].astype(jnp.bfloat16).reshape(attn_shape)
    values = (projected[:, 2] + bias_value).astype(jnp.bfloat16).reshape(attn_shape)
    positions = jnp.arange(seq_length, dtype=jnp.int32)
    inside = positions[None, :] < lengths[:, None]
    key_bias = jnp.where(inside, 0.0, -1000000000.0).astype(jnp.float32)

    def score_block():
        raw = jnp.einsum("sqhd,skhd->shqk", queries, keys, preferred_element_type=jnp.float32)
        return raw + key_bias[:, None, None, :]

    scores = score_block()
    peak = jnp.max(scores, axis=-1, keepdims=True)
    log_total = peak + jnp.log(jnp.sum(jnp.exp(scores - peak), axis=-1, keepdims=True))
    probs_low = jnp.exp(scores - log_total).astype(jnp.bfloat16)
    context_low = (
        jnp.einsum("shqk,skhd->sqhd", probs_low, values, preferred_element_type=jnp.float32)
        .reshape(row_count, head_cols)
        .astype(jnp.bfloat16)
    )
    attn_part = jnp.einsum("tc,dc->td", context_low, out_low, preferred_element_type=jnp.float32)
    attn_sum = lax.psum(attn_part, "tensor")
    residual_one = tokens_in.astype(jnp.float32) + attn_sum + biases[2]
    normed = layer_norm(residual_one, gains[0], biases[3])
    normed_low = normed.astype(jnp.bfloat16)
    pre_act = jnp.dot(normed_low, in_low, preferred_element_type=jnp.float32) + bias_hidden
    act_low = exact_gelu(pre_act).astype(jnp.bfloat16)
    down_part = jnp.einsum("tf,df->td", act_low, down_low, preferred_element_type=jnp.float32)
    down_sum = lax.psum(down_part, "tensor")
    residual_two = normed + down_sum + biases[4]
    live = inside.astype(jnp.int32) * span_mask.reshape(seq_count, seq_length) > 0
    upto = (positions[:, None] <= positions[None, :]).astype(jnp.float32)
    rank = jnp.dot(live.astype(jnp.float32), upto).astype(jnp.int32) - 1
    slots = jnp.arange(SPAN_ROWS, dtype=jnp.int32)
    pick = (live[:, None, :] & (rank[:, None, :] == slots[None, :, None])).astype(jnp.float32)
    pick_low = pick.astype(jnp.bfloat16)

    def rows_of(values):
        width = values.shape[-1]
        return jnp.einsum(
            "srt,std->srd",
            pick,
            values.reshape(seq_count, seq_length, width),
            precision=lax.Precision.HIGHEST,
        ).reshape(seq_count * SPAN_ROWS, width)

    def low_rows_of(values):
        width = values.shape[-1]
        return jnp.einsum(
            "srt,std->srd",
            pick_low,
            values.reshape(seq_count, seq_length, width),
            preferred_element_type=jnp.bfloat16,
        ).reshape(seq_count * SPAN_ROWS, width)

    result = layer_norm(residual_two, gains[1], biases[5])
    normed_out = result.astype(jnp.bfloat16)
    residual_one_rows = rows_of(residual_one)
    residual_two_rows = rows_of(residual_two)
    grad_result = low_rows_of(cotangent).astype(jnp.float32)
    _, norm_two_back = jax.vjp(layer_norm, residual_two_rows, gains[1], biases[5])
    d_res_two, d_gain_two, d_shift_two = norm_two_back(grad_result)
    d_res_two_low = d_res_two.astype(jnp.bfloat16)
    normed_low_rows = low_rows_of(normed_low)
    pre_rows = jnp.dot(normed_low_rows, in_low, preferred_element_type=jnp.float32) + bias_hidden
    act_rows, gelu_back = jax.vjp(exact_gelu, pre_rows)
    grad_back = outer_sum(d_res_two_low, act_rows.astype(jnp.bfloat16))
    d_act = jnp.dot(d_res_two_low, down_low, preferred_element_type=jnp.float32)
    d_pre = gelu_back(d_act)[0]
    d_pre_low = d_pre.astype(jnp.bfloat16)
    grad_in = outer_sum(normed_low_rows, d_pre_low)
    d_normed_part = jnp.einsum("tf,df->td", d_pre_low, in_low, preferred_element_type=jnp.float32)
    d_normed = lax.psum(d_normed_part, "tensor") + d_res_two
    _, norm_one_back = jax.vjp(layer_norm, residual_one_rows, gains[0], biases[3])
    d_res_one, d_gain_one, d_shift_one = norm_one_back(d_normed)
    d_res_one_low = d_res_one.astype(jnp.bfloat16)
    grad_out_proj = outer_sum(d_res_one_low, low_rows_of(context_low))
    row_shape = (seq_count, SPAN_ROWS, local_heads, head_size)
    d_context = (
        jnp.dot(d_res_one_low, out_low, preferred_element_type=jnp.float32)
        .astype(jnp.bfloat16)
        .reshape(row_shape)
    )
    query_rows = low_rows_of(queries.reshape(row_count, head_cols)).reshape(row_shape)
    raw = jnp.einsum("sqhd,skhd->shqk", query_rows, keys, preferred_element_type=jnp.float32)
    probs = jax.nn.softmax(raw + key_bias[:, None, None, :], axis=-1)
    probs_again = probs.astype(jnp.bfloat16)
    d_probs = jnp.einsum("sqhd,skhd->shqk", d_context, values, preferred_element_type=jnp.float32)
    d_values = jnp.einsum(
        "shqk,sqhd->skhd", probs_again, d_context, preferred_element_type=jnp.float32
    ).reshape(row_count, head_cols)
    d_scores = (probs * (d_probs - jnp.sum(probs * d_probs, axis=-1, keepdims=True))).astype(
        jnp.bfloat16
    )
    d_queries = (
        jnp.einsum("shqk,skhd->sqhd", d_scores, keys, preferred_element_type=jnp.float32).reshape(
            seq_count * SPAN_ROWS, head_cols
        )
        * query_scale
    )
    d_keys = jnp.einsum(
        "shqk,sqhd->skhd", d_scores, query_rows, preferred_element_type=jnp.float32
    ).reshape(row_count, head_cols)

    def spread(row_values):
        width = row_values.shape[-1]
        return jnp.einsum(
            "srt,srd->std",
            pick,
            row_values.reshape(seq_count, SPAN_ROWS, width),
            precision=lax.Precision.HIGHEST,
        ).reshape(row_count, width)

    d_proj_low = (
        jnp.stack([spread(d_queries), d_keys, d_values], axis=1)
        .astype(jnp.bfloat16)
        .reshape(row_count, 3 * head_cols)
    )
    grad_qkv = outer_sum(tokens_in, d_proj_low).reshape(model_width, 3, head_cols)
    d_entry_part = jnp.einsum("tc,dc->td", d_proj_low, qkv_low, preferred_element_type=jnp.float32)
    input_grad = lax.psum(d_entry_part, "tensor") + spread(d_res_one)
    first_rank = (tensor_slot == 0).astype(jnp.float32)
    width_zero = jnp.zeros((model_width,), jnp.float32)

    def place_heads(partial_sum):
        return lax.dynamic_update_slice_in_dim(width_zero, partial_sum, tensor_slot * head_cols, 0)

    grad_gains = jnp.stack([d_gain_one, d_gain_two]) * first_rank
    grad_biases = jnp.stack(
        [
            place_heads(jnp.sum(d_queries, axis=0)),
            place_heads(jnp.sum(d_values, axis=0)),
            jnp.sum(d_res_one, axis=0) * first_rank,
            d_shift_one * first_rank,
            jnp.sum(d_res_two, axis=0) * first_rank,
            d_shift_two * first_rank,
        ]
    )
    grad_bias_in = lax.dynamic_update_slice_in_dim(
        jnp.zeros(bias_in.shape, jnp.float32), jnp.sum(d_pre, axis=0), tensor_slot * hidden_cols, 0
    )
    grad_gains, grad_biases, grad_bias_in = lax.psum(
        (grad_gains, grad_biases, grad_bias_in), ("dp", "tensor")
    )
    data_slot = lax.axis_index("dp")
    shard_rows = model_width // lax.axis_size("dp")
    owned = tuple(
        (
            lax.psum_scatter(part, "dp", scatter_dimension=0, tiled=True)
            for part in (grad_qkv, grad_out_proj, grad_in, grad_back)
        )
    )
    clock = step[0].astype(jnp.float32)
    warm = warmup[0].astype(jnp.float32)
    horizon = total[0].astype(jnp.float32)
    ratio = jnp.minimum(clock / warm, (horizon - clock) / (horizon - warm))
    corr_one = 1.0 - jnp.power(BETA_ONE, clock)
    corr_two = 1.0 - jnp.power(BETA_TWO, clock)
    change_rows = []
    fresh_moments = []
    for weight, grad_rows, moment in zip(
        (w_qkv, w_out, w_in, w_back), owned, (mom_qkv, mom_out, mom_in, mom_back)
    ):
        weight_rows = lax.dynamic_slice_in_dim(weight, data_slot * shard_rows, shard_rows, 0)
        row_change, new_moment = adam_step(
            weight_rows, grad_rows, moment, ratio, corr_one, corr_two, WEIGHT_DECAY
        )
        change_rows.append(row_change)
        fresh_moments.append(new_moment)
    change_qkv, change_out_proj, change_in_proj, change_back_proj = (
        lax.all_gather(change_rows[0], "dp", axis=0, tiled=True),
        lax.all_gather(change_rows[1], "dp", axis=0, tiled=True),
        lax.all_gather(change_rows[2], "dp", axis=0, tiled=True),
        lax.all_gather(change_rows[3], "dp", axis=0, tiled=True),
    )
    change_gains, new_mom_gains = adam_step(
        gains, grad_gains, mom_gains, ratio, corr_one, corr_two, 0.0
    )
    change_biases, new_mom_biases = adam_step(
        biases, grad_biases, mom_biases, ratio, corr_one, corr_two, 0.0
    )
    change_bias_in, new_mom_bias_in = adam_step(
        bias_in, grad_bias_in, mom_bias_in, ratio, corr_one, corr_two, 0.0
    )
    return (
        normed_out,
        input_grad,
        change_qkv,
        change_out_proj,
        change_in_proj,
        change_back_proj,
        change_gains,
        change_biases,
        change_bias_in,
        fresh_moments[0],
        fresh_moments[1],
        fresh_moments[2],
        fresh_moments[3],
        new_mom_gains,
        new_mom_biases,
        new_mom_bias_in,
    )


def solution(mesh):
    in_specs = (
        P("dp", None),
        P("dp", None),
        P("dp"),
        P("dp"),
        P(),
        P(),
        P(),
        P(None, None, "tensor"),
        P(None, "tensor"),
        P(None, "tensor"),
        P(None, "tensor"),
        P(),
        P(),
        P(),
        P(None, "dp", None, "tensor"),
        P(None, "dp", "tensor"),
        P(None, "dp", "tensor"),
        P(None, "dp", "tensor"),
        P(),
        P(),
        P(),
    )
    out_specs = (
        P("dp", None),
        P("dp", None),
        P(None, None, "tensor"),
        P(None, "tensor"),
        P(None, "tensor"),
        P(None, "tensor"),
        P(),
        P(),
        P(),
        P(None, "dp", None, "tensor"),
        P(None, "dp", "tensor"),
        P(None, "dp", "tensor"),
        P(None, "dp", "tensor"),
        P(),
        P(),
        P(),
    )
    return jax.shard_map(
        on_device, mesh=mesh, in_specs=in_specs, out_specs=out_specs, check_vma=False
    )
```

profile of v0, /device:TPU:0, one launch (start us, length us, event | category | flops | bytes accessed | tf_op | source)
XLA Modules:
  0.0 894.0 jit_solution(5073173420024962855)
XLA Ops:
  7.2 3.9 fusion.15
  13.9 2.1 convert_element_type.129
  16.0 1.7 squeeze.7
  18.3 1.8 fusion.168
  20.9 1.8 multiply_convert_fusion
  22.7 2.8 add_reduce_fusion
  25.6 1.8 exponential_reduce_fusion
  27.3 1.8 copy-done.3
  29.8 2.8 squeeze.6
  32.7 1.8 add_convert_fusion.1
  34.5 5.7 fusion.20
  41.2 3.0 fusion.96
  46.6 94.5 %all-reduce.6.cloned.1.call-done = f32[1536,768]{1,0:T(8,128)} async-done(((f32[1536,768]{1,0:T(8,128)}), f32[1536,768]{1,0:T(8,128)}) %all-reduce.6.cloned.1.call-update) | async-done | bytes 4718608 | tf_op jit(solution)/shard_map/psum | solution.py:103
  141.1 3.8 fusion.167
  145.7 1.4 copy-done.2
  147.1 2.1 fusion.14
  149.2 17.8 %fusion.18 = f32[1536,768]{1,0:T(8,128)} fusion(bf16[1536,768]{1,0:T(8,128)(2,1)} %fusion.14, f32[768]{0:T(1024)} %dynamic_slice.23, f32[768,768]{1,0:T(8,128)} %param.31, f32[768,768]{1,0:T(8,128)} %param.30), kind=kOutput, calls=%fused_computation.39 | convolution fusion | flops 3702915072 | bytes 11799552 | tf_op jit(solution)/shard_map/tf,df->td/dot_general | solution.py:109
  167.2 1.8 squeeze.8
  170.6 2.0 fusion.35
  172.6 3.1 fusion.175
  175.7 4.6 fusion.173
  183.3 78.0 %all-reduce.8.cloned.1.call-done = f32[1536,768]{1,0:T(8,128)} async-done(((f32[1536,768]{1,0:T(8,128)}), f32[1536,768]{1,0:T(8,128)}) %all-reduce.8.cloned.1.call-update) | async-done | bytes 4718608 | tf_op jit(solution)/shard_map/psum | solution.py:110
  261.3 5.3 fusion.166
  266.7 2.2 copy-done.4
  268.9 2.1 fusion.174
  271.0 2.0 multiply_reduce_fusion.8
  273.2 1.4 fusion.100
  274.8 1.4 fusion.25
  276.3 4.8 fusion.180
  283.3 33.8 %all-reduce.10.cloned.1.call-done = f32[240,768]{1,0:T(8,128)} async-done(((f32[240,768]{1,0:T(8,128)}), f32[240,768]{1,0:T(8,128)}) %all-reduce.10.cloned.1.call-update) | async-done | bytes 737296 | tf_op jit(solution)/shard_map/psum | solution.py:154
  317.0 2.2 fusion.163
  320.9 1.5 convolution_convert_fusion.1
  323.2 2.6 fusion.179
  327.9 1.7 fusion.178
  330.9 1.8 copy.94
  332.7 1.5 stack_reshape.10
  334.2 1.6 fusion.49
  336.3 1.5 stack_reshape.9
  337.9 1.4 maximum_convert_fusion
  339.3 4.4 fusion.181
  343.7 3.0 copy.97
  346.8 1.9 fusion.89
  348.8 4.6 fusion.62
  355.3 6.1 convolution_bitcast_fusion
  365.0 51.3 %reduce-scatter.5.cloned.1.call-done = f32[96,3,192]{2,0,1:T(8,128)} async-done(((f32[768,3,192]{2,0,1:T(8,128)}), f32[96,3,192]{2,0,1:T(8,128)}) %reduce-scatter.5.cloned.1.call-update) | async-done | bytes 221200 | tf_op jit(solution)/shard_map/reduce_scatter | solution.py:230
  416.3 2.2 fusion.104
  418.5 69.8 %reduce-scatter.9.cloned.1.call-done = f32[96,768]{1,0:T(8,128)} async-done(((f32[768,768]{1,0:T(8,128)}), f32[96,768]{1,0:T(8,128)}) %reduce-scatter.9.cloned.1.call-update) | async-done | bytes 294928 | tf_op jit(solution)/shard_map/reduce_scatter | solution.py:230
  488.3 2.2 fusion.105
  492.8 3.0 multiply_reduce_fusion
  495.9 4.2 add_convert_fusion
  500.1 59.7 %reduce-scatter.11.cloned.1.call-done = f32[96,768]{1,0:T(8,128)} async-done(((f32[768,768]{1,0:T(8,128)}), f32[96,768]{1,0:T(8,128)}) %reduce-scatter.11.cloned.1.call-update) | async-done | bytes 294928 | tf_op jit(solution)/shard_map/reduce_scatter | solution.py:230
  559.9 2.0 fusion.106
  562.9 40.3 %all-reduce = (f32[2,768]{1,0:T(2,128)S(1)}, f32[6,768]{1,0:T(8,128)S(1)}, f32[3072]{0:T(1024)S(1)}) all-reduce(f32[2,768]{1,0:T(2,128)S(1)} %maximum_multiply_fusion, f32[6,768]{1,0:T(8,128)S(1)} %stack.88, f32[3072]{0:T(1024)S(1)} %dynamic_update_slice.13), channel_id=1, replica_groups=mesh['dp'=8,'tensor'=4] {'dp','tensor'}, use_global_device_ids=true, to_apply=%region_27.28 | all-reduce | flops 9216 | bytes 73728 | tf_op jit(solution)/shard_map/psum | solution.py:223
  607.0 4.3 fusion.47
  611.3 13.9 %reduce-scatter.7.cloned.1.call-done = f32[96,192]{1,0:T(8,128)} async-done(((f32[768,192]{1,0:T(8,128)}), f32[96,192]{1,0:T(8,128)}) %reduce-scatter.7.cloned.1.call-update) | async-done | bytes 73744 | tf_op jit(solution)/shard_map/reduce_scatter | solution.py:230
  626.3 32.2 %all_gather.13 = f32[768,192]{1,0:T(8,128)S(1)} all-gather(f32[96,192]{1,0:T(8,128)S(1)} %get-tuple-element.107), channel_id=1, replica_groups=mesh['dp'=8,'tensor'=4] {'dp'}, dimensions={0}, use_global_device_ids=true | all-gather | bytes 663552 | tf_op jit(solution)/shard_map/all_gather | solution.py:253
  660.3 60.5 %all-reduce.12.cloned.1.call-done = f32[1536,768]{1,0:T(8,128)} async-done(((f32[1536,768]{1,0:T(8,128)}), f32[1536,768]{1,0:T(8,128)}) %all-reduce.12.cloned.1.call-update) | async-done | bytes 4718608 | tf_op jit(solution)/shard_map/psum | solution.py:202
  720.8 6.6 bitcast_add_fusion
  729.9 46.0 %all-gather.4.cloned.1.call-done = f32[768,3,192]{2,0,1:T(8,128)} async-done(((f32[96,3,192]{2,0,1:T(8,128)}), f32[768,3,192]{2,0,1:T(8,128)}) %all-gather.4.cloned.1.call-update) | async-done | bytes 1769488 | tf_op jit(solution)/shard_map/all_gather | solution.py:252
  775.9 2.9 copy.102
  778.8 50.6 %all-gather.6.cloned.1.call-done = f32[768,768]{1,0:T(8,128)} async-done(((f32[96,768]{1,0:T(8,128)}), f32[768,768]{1,0:T(8,128)}) %all-gather.6.cloned.1.call-update) | async-done | bytes 2359312 | tf_op jit(solution)/shard_map/all_gather | solution.py:254
  829.4 53.1 %all-gather.8.cloned.1.call-done = f32[768,768]{1,0:T(8,128)} async-done(((f32[96,768]{1,0:T(8,128)}), f32[768,768]{1,0:T(8,128)}) %all-gather.8.cloned.1.call-update) | async-done | bytes 2359312 | tf_op jit(solution)/shard_map/all_gather | solution.py:255
  882.5 3.4 copy.181
  885.9 1.4 copy.182
  (237 shorter events, 38.6 us)
Async XLA Ops:
  7.2 263.8 %copy-start = (bf16[1536,768]{1,0:T(8,128)(2,1)S(1)}, bf16[1536,768]{1,0:T(8,128)(2,1)}, u32[]{:S(2)}) copy-start(bf16[1536,768]{1,0:T(8,128)(2,1)} %param.22) | copy-start | bytes 7077892
  7.2 133.9 %all-reduce.6.cloned.1.call-start = ((), (), s32[]{:S(2)}) async-start(), calls=%async_computation.4 | async-start | bytes 9437184 | tf_op jit(solution)/shard_map/psum | solution.py:103
  11.2 2.7 copy-start.63
  25.5 3.6 copy-start.3
  25.5 7.0 copy-start.60
  34.4 5.7 copy-start.15
  34.4 6.7 copy-start.19
  44.2 217.1 %all-reduce.8.cloned.1.call-start = ((), (), s32[]{:S(2)}) async-start(), calls=%async_computation.5 | async-start | bytes 9437184 | tf_op jit(solution)/shard_map/psum | solution.py:110
  144.9 2.2 copy-start.2
  167.0 150.0 %all-reduce.10.cloned.1.call-start = ((), (), s32[]{:S(2)}) async-start(), calls=%async_computation.6 | async-start | bytes 1474560 | tf_op jit(solution)/shard_map/psum | solution.py:154
  172.6 9.3 %copy-start.26 = (bf16[3,80,192]{1,2,0:T(8,128)(2,1)}, bf16[3,80,192]{1,2,0:T(8,128)(2,1)S(1)}, u32[]{:S(2)}) copy-start(bf16[3,80,192]{1,2,0:T(8,128)(2,1)S(1)} %fusion.35) | copy-start | bytes 276484
  175.7 5.7 copy-start.10
  175.7 6.2 copy-start.8
  175.7 6.2 copy-start.55
  180.3 81.0 %copy-start.31 = (f32[1536]{0:T(1024)S(1)}, f32[1536]{0:T(1024)}, u32[]{:S(2)}) copy-start(f32[1536]{0:T(1024)} %copy-done.30) | copy-start | bytes 18436
  180.3 81.0 %copy-start.35 = (f32[1536]{0:T(1024)S(1)}, f32[1536]{0:T(1024)}, u32[]{:S(2)}) copy-start(f32[1536]{0:T(1024)} %copy-done.34) | copy-start | bytes 18436
  180.3 81.0 %copy-start.40 = (f32[768]{0:T(1024)S(1)}, f32[768]{0:T(1024)}, u32[]{:S(2)}) copy-start(f32[768]{0:T(1024)} %get-tuple-element.118) | copy-start | bytes 9220
  180.3 81.0 %copy-start.57 = (f32[768]{0:T(1024)S(1)}, f32[768]{0:T(1024)}, u32[]{:S(2)}) copy-start(f32[768]{0:T(1024)} %get-tuple-element.119) | copy-start | bytes 9220
  266.7 2.2 copy-start.4
  273.2 7.9 copy-start.45
  273.2 7.9 copy-start.47
  274.6 6.4 copy-start.49
  276.3 4.8 copy-start.17
  276.3 4.8 copy-start.9
  281.0 2.2 copy-start.23
  282.5 133.8 %reduce-scatter.5.cloned.1.call-start = ((), (), s32[]{:S(2)}) async-start(), calls=%async_computation.8 | async-start | bytes 2654208 | tf_op jit(solution)/shard_map/reduce_scatter | solution.py:230
  320.9 4.9 copy-start.11
  323.2 2.6 copy-start.16
  323.2 2.6 copy-start.29
  330.9 8.4 copy-start.21
  343.7 3.1 copy-start.24
  346.7 141.6 %reduce-scatter.9.cloned.1.call-start = ((), (), s32[]{:S(2)}) async-start(), calls=%async_computation.11 | async-start | bytes 2654208 | tf_op jit(solution)/shard_map/reduce_scatter | solution.py:230
  348.8 4.7 copy-start.14
  348.8 211.1 %reduce-scatter.11.cloned.1.call-start = ((), (), s32[]{:S(2)}) async-start(), calls=%async_computation.13 | async-start | bytes 2654208 | tf_op jit(solution)/shard_map/reduce_scatter | solution.py:230
  353.4 271.8 %reduce-scatter.7.cloned.1.call-start = ((), (), s32[]{:S(2)}) async-start(), calls=%async_computation.10 | async-start | bytes 884736 | tf_op jit(solution)/shard_map/reduce_scatter | solution.py:230
  355.0 365.8 %all-reduce.12.cloned.1.call-start = ((), (), s32[]{:S(2)}) async-start(), calls=%async_computation.7 | async-start | bytes 9437184 | tf_op jit(solution)/shard_map/psum | solution.py:202
  361.3 130.4 %copy-start.38 = (f32[2,6,768]{2,0,1:T(2,128)S(1)}, f32[2,6,768]{2,0,1:T(2,128)}, u32[]{:S(2)}) copy-start(f32[2,6,768]{2,0,1:T(2,128)} %param.40) | copy-start | bytes 110596
  361.3 130.4 %copy-start.42 = (f32[2,3072]{1,0:T(2,128)S(1)}, f32[2,3072]{1,0:T(2,128)}, u32[]{:S(2)}) copy-start(f32[2,3072]{1,0:T(2,128)} %param.41) | copy-start | bytes 73732
  361.3 131.0 %copy-start.7 = (f32[3,80,768]{2,1,0:T(8,128)S(1)}, f32[3,80,768]{2,1,0:T(8,128)}, u32[]{:S(2)}) copy-start(f32[3,80,768]{2,1,0:T(8,128)} %get-tuple-element.137) | copy-start | bytes 2211844
  361.3 131.0 %copy-start.46 = (f32[3,80]{1,0:T(4,128)S(1)}, f32[3,80]{1,0:T(4,128)}, u32[]{:S(2)}) copy-start(f32[3,80]{1,0:T(4,128)} %copy-done.45) | copy-start | bytes 2884
  361.3 131.0 %copy-start.48 = (f32[3,80]{1,0:T(4,128)S(1)}, f32[3,80]{1,0:T(4,128)}, u32[]{:S(2)}) copy-start(f32[3,80]{1,0:T(4,128)} %copy-done.47) | copy-start | bytes 2884
  361.3 131.0 %copy-start.50 = (f32[3,80]{1,0:T(4,128)S(1)}, f32[3,80]{1,0:T(4,128)}, u32[]{:S(2)}) copy-start(f32[3,80]{1,0:T(4,128)} %copy-done.49) | copy-start | bytes 2884
  361.4 131.4 %copy-start.41 = (f32[1536]{0:T(1024)S(1)}, f32[1536]{0:T(1024)}, u32[]{:S(2)}) copy-start(f32[1536]{0:T(1024)} %get-tuple-element.88) | copy-start | bytes 18436
  361.4 414.5 %all-gather.4.cloned.1.call-start = ((), (), s32[]{:S(2)}) async-start(), calls=%async_computation.9 | async-start | bytes 2654208 | tf_op jit(solution)/shard_map/all_gather | solution.py:252
  418.4 77.3 %copy-start.51 = (f32[768]{0:T(1024)S(1)}, f32[768]{0:T(1024)}, u32[]{:S(2)}) copy-start(f32[768]{0:T(1024)} %get-tuple-element.120) | copy-start | bytes 9220
  418.5 410.9 %all-gather.6.cloned.1.call-start = ((), (), s32[]{:S(2)}) async-start(), calls=%async_computation.12 | async-start | bytes 2654208 | tf_op jit(solution)/shard_map/all_gather | solution.py:254
  490.5 392.0 %all-gather.8.cloned.1.call-start = ((), (), s32[]{:S(2)}) async-start(), calls=%async_computation.14 | async-start | bytes 2654208 | tf_op jit(solution)/shard_map/all_gather | solution.py:255
  495.7 64.1 %copy-start.28 = (f32[2,96,768]{2,1,0:T(8,128)S(1)}, f32[2,96,768]{2,1,0:T(8,128)}, u32[]{:S(2)}) copy-start(f32[2,96,768]{2,1,0:T(8,128)} %param.38) | copy-start | bytes 1769476
  495.8 66.1 %copy-start.56 = (f32[768]{0:T(1024)S(1)}, f32[768]{0:T(1024)}, u32[]{:S(2)}) copy-start(f32[768]{0:T(1024)} %get-tuple-element.70) | copy-start | bytes 9220
  495.8 66.2 %copy-start.59 = (f32[768]{0:T(1024)S(1)}, f32[768]{0:T(1024)}, u32[]{:S(2)}) copy-start(f32[768]{0:T(1024)} %get-tuple-element.146) | copy-start | bytes 9220
  495.8 66.5 %copy-start.52 = (f32[768]{0:T(1024)S(1)}, f32[768]{0:T(1024)}, u32[]{:S(2)}) copy-start(f32[768]{0:T(1024)} %get-tuple-element.66) | copy-start | bytes 9220
  495.8 66.5 %copy-start.62 = (f32[3,64]{1,0:T(4,128)S(1)}, f32[3,64]{1,0:T(4,128)}, u32[]{:S(2)}) copy-start(f32[3,64]{1,0:T(4,128)} %get-tuple-element.142) | copy-start | bytes 2308
  495.8 66.5 %copy-start.61 = (f32[3,64]{1,0:T(4,128)S(1)}, f32[3,64]{1,0:T(4,128)}, u32[]{:S(2)}) copy-start(f32[3,64]{1,0:T(4,128)} %get-tuple-element.144) | copy-start | bytes 2308
  495.8 66.6 %copy-start.54 = (f32[768]{0:T(1024)S(1)}, f32[768]{0:T(1024)}, u32[]{:S(2)}) copy-start(f32[768]{0:T(1024)} %get-tuple-element.85) | copy-start | bytes 9220
  495.8 66.6 %copy-start.53 = (f32[768]{0:T(1024)S(1)}, f32[768]{0:T(1024)}, u32[]{:S(2)}) copy-start(f32[768]{0:T(1024)} %get-tuple-element.71) | copy-start | bytes 9220
  495.9 107.4 %copy-start.33 = (f32[6,768]{1,0:T(8,128)S(1)}, f32[6,768]{1,0:T(8,128)}, u32[]{:S(2)}) copy-start(f32[6,768]{1,0:T(8,128)} %param.33) | copy-start | bytes 55300
  495.9 108.7 %copy-start.43 = (f32[2,768]{1,0:T(2,128)S(1)}, f32[2,768]{1,0:T(2,128)}, u32[]{:S(2)}) copy-start(f32[2,768]{1,0:T(2,128)} %param.32) | copy-start | bytes 18436
  495.9 108.7 %copy-start.58 = (f32[2,2,768]{2,1,0:T(2,128)S(1)}, f32[2,2,768]{2,1,0:T(2,128)}, u32[]{:S(2)}) copy-start(f32[2,2,768]{2,1,0:T(2,128)} %param.39) | copy-start | bytes 36868
  495.9 109.9 %copy-start.36 = (f32[1,3072]{1,0:T(1,128)S(1)}, f32[1,3072]{1,0:T(1,128)}, u32[]{:S(2)}) copy-start(f32[1,3072]{1,0:T(1,128)} %get-tuple-element.113) | copy-start | bytes 36868
  495.9 109.9 %copy-start.37 = (f32[1,3072]{1,0:T(1,128)S(1)}, f32[1,3072]{1,0:T(1,128)}, u32[]{:S(2)}) copy-start(f32[1,3072]{1,0:T(1,128)} %get-tuple-element.114) | copy-start | bytes 36868
  495.9 109.9 %copy-start.44 = (f32[3072]{0:T(1024)S(1)}, f32[3072]{0:T(1024)}, u32[]{:S(2)}) copy-start(f32[3072]{0:T(1024)} %param.34) | copy-start | bytes 36868
  660.3 67.1 %copy-start.25 = (f32[1,96,3,192]{3,1,2,0:T(8,128)S(1)}, f32[1,96,3,192]{3,1,2,0:T(8,128)}, u32[]{:S(2)}) copy-start(f32[1,96,3,192]{3,1,2,0:T(8,128)} %get-tuple-element.103) | copy-start | bytes 663556
  882.5 3.4 copy-start.20
  882.5 4.8 copy-start.1
  (11 other events, 18.4 us)
Sparse Core Ops, SparseCore 0:
  44.3 96.7 all-reduce.5
  167.1 94.1 all-reduce.7
  282.6 34.3 all-reduce.9
  346.9 69.3 reduce-scatter.4
  420.2 68.0 reduce-scatter.8
  491.6 68.1 reduce-scatter.10
  563.7 61.4 reduce-scatter.6
  627.8 92.9 all-reduce.11
  723.8 52.0 all-gather.3
  778.8 50.5 all-gather.5
  831.8 50.5 all-gather.7
where the time goes:
time: 903 us; the launch traced here: 894 us
  waiting for transfers between devices  611 us (68%)
  matrix products  86.9 us (10%)
  blocking collectives  72.5 us (8%)
  other arithmetic  56.1 us (6%)
  local copies, waits for them, and re-layouts  48.5 us (5%)
  between operations  17.2 us (2%)
    reduce_scatter x4, waiting for transfers between devices, on_device(): lax.psum_scatter(part, 'dp', scatter_dimension=0, tiled=True)  195 us
    psum x1, waiting for transfers between devices, on_device(): attn_sum = lax.psum(attn_part, 'tensor')  94.5 us
    psum x1, waiting for transfers between devices, on_device(): down_sum = lax.psum(down_part, 'tensor')  78 us
    psum x1, waiting for transfers between devices, on_device(): input_grad = lax.psum(d_entry_part, 'tensor') + spread(d_res_one)  60.5 us
    all_gather x1, waiting for transfers between devices, on_device(): lax.all_gather(change_rows[3], 'dp', axis=0, tiled=True)  53.1 us
    all_gather x1, waiting for transfers between devices, on_device(): lax.all_gather(change_rows[2], 'dp', axis=0, tiled=True)  50.6 us
    all_gather x1, waiting for transfers between devices, on_device(): lax.all_gather(change_rows[0], 'dp', axis=0, tiled=True)  46 us
    psum x1, blocking collectives, on_device(): lax.psum((grad_gains, grad_biases, grad_bias_in), ('dp', 'tensor'))  40.3 us
  transfers between devices with their start and end apart: 11, of which 11 were waited for; matrix products, arithmetic and copies ran while one was open for 8% of the time, Pallas kernels for 0%

commit v1 on v0

--- a/solution.py
+++ b/solution.py
@@ -11,6 +11,28 @@
 BETA_TWO = 0.999
 ADAM_EPS = 1e-06
 WEIGHT_DECAY = 0.01
+
+
+def in_order(parts, dim):
+    lengths = list(parts.shape[1:])
+    lengths[dim] *= parts.shape[0]
+    return jnp.moveaxis(parts, 0, dim).reshape(lengths)
+
+
+def grow_blocks(shard, axis):
+    size = lax.axis_size(axis)
+    tiles = shard[None]
+    for level in range(size.bit_length() - 1):
+        apart = 1 << level
+        received = lax.ppermute(tiles, axis, [(i, i ^ apart) for i in range(size)])
+        both = jnp.stack([tiles, received])
+        upper = lax.axis_index(axis) >> level & 1
+        tiles = jnp.where(upper == 0, both, both[::-1]).reshape(-1, *shard.shape)
+    return tiles
+
+
+def doubled_up(array, axis, dim):
+    return in_order(grow_blocks(array, axis), dim)
 
 
 def layer_norm(values, gain, shift):
@@ -252,7 +274,7 @@
         lax.all_gather(change_rows[0], "dp", axis=0, tiled=True),
         lax.all_gather(change_rows[1], "dp", axis=0, tiled=True),
         lax.all_gather(change_rows[2], "dp", axis=0, tiled=True),
-        lax.all_gather(change_rows[3], "dp", axis=0, tiled=True),
+        doubled_up(change_rows[3], "dp", 0),
     )
     change_gains, new_mom_gains = adam_step(
         gains, grad_gains, mom_gains, ratio, corr_one, corr_two, 0.0

time: 903 us -> 847 us (0.938)
  waiting for transfers between devices: 611 us -> 554 us
    all_gather x1 -> x0, waiting for transfers between devices: 53.1 us -> none  [on_device(): lax.all_gather(change_rows[3], 'dp', axis=0, tiled=True)]
  transfers between devices with their start and end apart: 11 -> 13, of which waited for: 11 -> 11; matrix products, arithmetic and copies ran while one was open for 8% -> 9% of each run, Pallas kernels for 0% -> 0%
where the time goes in v1:
time: 847 us; the launch traced here: 838 us
  waiting for transfers between devices  554 us (65%)
  matrix products  85.8 us (10%)
  blocking collectives  73.3 us (9%)
  other arithmetic  57 us (7%)
  local copies, waits for them, and re-layouts  47.5 us (6%)
  between operations  17.5 us (2%)
    reduce_scatter x4, waiting for transfers between devices, on_device(): lax.psum_scatter(part, 'dp', scatter_dimension=0, tiled=True)  188 us
    psum x1, waiting for transfers between devices, on_device(): attn_sum = lax.psum(attn_part, 'tensor')  94.5 us
    psum x1, waiting for transfers between devices, on_device(): down_sum = lax.psum(down_part, 'tensor')  78 us
    psum x1, waiting for transfers between devices, on_device(): input_grad = lax.psum(d_entry_part, 'tensor') + spread(d_res_one)  59 us
    all_gather x1, waiting for transfers between devices, on_device(): lax.all_gather(change_rows[2], 'dp', axis=0, tiled=True)  50.6 us
    all_gather x1, waiting for transfers between devices, on_device(): lax.all_gather(change_rows[0], 'dp', axis=0, tiled=True)  43.6 us
    psum x1, blocking collectives, on_device(): lax.psum((grad_gains, grad_biases, grad_bias_in), ('dp', 'tensor'))  40.9 us
    psum x1, waiting for transfers between devices, on_device(): d_normed = lax.psum(d_normed_part, 'tensor') + d_res_two  33.8 us
  transfers between devices with their start and end apart: 13, of which 11 were waited for; matrix products, arithmetic and copies ran while one was open for 9% of the time, Pallas kernels for 0%

profile of v1, /device:TPU:0, one launch (start us, length us, event | category | flops | bytes accessed | tf_op | source)
XLA Modules:
  0.0 837.9 jit_solution(15101758254510077992)
XLA Ops:
  7.2 3.9 fusion.15
  13.9 2.1 convert_element_type.129
  16.0 1.7 squeeze.7
  18.3 1.8 fusion.170
  20.9 1.8 multiply_convert_fusion
  22.7 2.8 add_reduce_fusion
  25.6 1.8 exponential_reduce_fusion
  27.3 1.9 copy-done.3
  29.8 2.8 squeeze.6
  32.7 1.8 add_convert_fusion.1
  34.5 5.7 fusion.20
  41.2 3.0 fusion.98
  44.5 1.4 dynamic_slice.23
  46.6 94.5 %all-reduce.6.cloned.1.call-done = f32[1536,768]{1,0:T(8,128)} async-done(((f32[1536,768]{1,0:T(8,128)}), f32[1536,768]{1,0:T(8,128)}) %all-reduce.6.cloned.1.call-update) | async-done | bytes 4718608 | tf_op jit(solution)/shard_map/psum | solution.py:125
  141.1 3.8 fusion.169
  145.7 1.4 copy-done.2
  147.1 2.1 fusion.14
  149.2 17.8 %fusion.18 = f32[1536,768]{1,0:T(8,128)} fusion(bf16[1536,768]{1,0:T(8,128)(2,1)} %fusion.14, f32[768]{0:T(1024)} %dynamic_slice.23, f32[768,768]{1,0:T(8,128)} %param.31, f32[768,768]{1,0:T(8,128)} %param.30), kind=kOutput, calls=%fused_computation.42 | convolution fusion | flops 3702915072 | bytes 11799552 | tf_op jit(solution)/shard_map/tf,df->td/dot_general | solution.py:131
  167.3 1.8 squeeze.8
  170.6 2.0 fusion.35
  172.6 3.1 fusion.177
  175.7 4.6 fusion.175
  183.3 78.0 %all-reduce.8.cloned.1.call-done = f32[1536,768]{1,0:T(8,128)} async-done(((f32[1536,768]{1,0:T(8,128)}), f32[1536,768]{1,0:T(8,128)}) %all-reduce.8.cloned.1.call-update) | async-done | bytes 4718608 | tf_op jit(solution)/shard_map/psum | solution.py:132
  261.3 4.7 fusion.168
  266.1 2.2 copy-done.4
  268.3 2.1 fusion.176
  270.4 2.0 multiply_reduce_fusion.8
  272.6 1.4 fusion.102
  274.2 1.4 fusion.25
  275.7 4.8 fusion.182
  280.4 1.4 fusion.93
  282.6 33.8 %all-reduce.10.cloned.1.call-done = f32[240,768]{1,0:T(8,128)} async-done(((f32[240,768]{1,0:T(8,128)}), f32[240,768]{1,0:T(8,128)}) %all-reduce.10.cloned.1.call-update) | async-done | bytes 737296 | tf_op jit(solution)/shard_map/psum | solution.py:176
  316.4 2.2 fusion.165
  320.3 1.5 convolution_convert_fusion.1
  322.6 2.0 fusion.181
  329.1 1.8 copy.94
  330.9 1.5 stack_reshape.16
  332.5 1.6 fusion.51
  334.6 1.5 stack_reshape.15
  336.1 1.4 maximum_convert_fusion
  337.6 4.4 fusion.183
  342.0 3.0 copy.97
  345.0 1.9 fusion.91
  347.1 4.6 fusion.64
  353.5 6.1 convolution_bitcast_fusion
  365.9 48.6 %reduce-scatter.5.cloned.1.call-done = f32[96,3,192]{2,0,1:T(8,128)} async-done(((f32[768,3,192]{2,0,1:T(8,128)}), f32[96,3,192]{2,0,1:T(8,128)}) %reduce-scatter.5.cloned.1.call-update) | async-done | bytes 221200 | tf_op jit(solution)/shard_map/reduce_scatter | solution.py:252
  414.5 2.1 fusion.106
  416.7 3.0 multiply_reduce_fusion
  419.8 4.0 add_convert_fusion
  424.4 40.9 %all-reduce = (f32[2,768]{1,0:T(2,128)S(1)}, f32[6,768]{1,0:T(8,128)S(1)}, f32[3072]{0:T(1024)S(1)}) all-reduce(f32[2,768]{1,0:T(2,128)S(1)} %maximum_multiply_fusion, f32[6,768]{1,0:T(8,128)S(1)} %stack.112, f32[3072]{0:T(1024)S(1)} %dynamic_update_slice.13), channel_id=1, replica_groups=mesh['dp'=8,'tensor'=4] {'dp','tensor'}, use_global_device_ids=true, to_apply=%region_27.28 | all-reduce | flops 9216 | bytes 73728 | tf_op jit(solution)/shard_map/psum | solution.py:245
  468.5 18.8 %reduce-scatter.9.cloned.1.call-done = f32[96,768]{1,0:T(8,128)} async-done(((f32[768,768]{1,0:T(8,128)}), f32[96,768]{1,0:T(8,128)}) %reduce-scatter.9.cloned.1.call-update) | async-done | bytes 294928 | tf_op jit(solution)/shard_map/reduce_scatter | solution.py:252
  487.2 2.0 fusion.107
  489.3 4.3 fusion.49
  493.6 65.0 %reduce-scatter.11.cloned.1.call-done = f32[96,768]{1,0:T(8,128)} async-done(((f32[768,768]{1,0:T(8,128)}), f32[96,768]{1,0:T(8,128)}) %reduce-scatter.11.cloned.1.call-update) | async-done | bytes 294928 | tf_op jit(solution)/shard_map/reduce_scatter | solution.py:252
  561.2 6.3 collective-permute-done
  568.4 55.7 %reduce-scatter.7.cloned.1.call-done = f32[96,192]{1,0:T(8,128)} async-done(((f32[768,192]{1,0:T(8,128)}), f32[96,192]{1,0:T(8,128)}) %reduce-scatter.7.cloned.1.call-update) | async-done | bytes 73744 | tf_op jit(solution)/shard_map/reduce_scatter | solution.py:252
  625.2 32.4 %all_gather.10 = f32[768,192]{1,0:T(8,128)S(1)} all-gather(f32[96,192]{1,0:T(8,128)S(1)} %get-tuple-element.109), channel_id=1, replica_groups=mesh['dp'=8,'tensor'=4] {'dp'}, dimensions={0}, use_global_device_ids=true | all-gather | bytes 663552 | tf_op jit(solution)/shard_map/all_gather | solution.py:275
  660.7 59.0 %all-reduce.12.cloned.1.call-done = f32[1536,768]{1,0:T(8,128)} async-done(((f32[1536,768]{1,0:T(8,128)}), f32[1536,768]{1,0:T(8,128)}) %all-reduce.12.cloned.1.call-update) | async-done | bytes 4718608 | tf_op jit(solution)/shard_map/psum | solution.py:224
  719.7 6.6 bitcast_add_fusion
  729.0 1.6 reverse_select_fusion
  730.6 43.6 %all-gather.3.cloned.1.call-done = f32[768,3,192]{2,0,1:T(8,128)} async-done(((f32[96,3,192]{2,0,1:T(8,128)}), f32[768,3,192]{2,0,1:T(8,128)}) %all-gather.3.cloned.1.call-update) | async-done | bytes 1769488 | tf_op jit(solution)/shard_map/all_gather | solution.py:274
  774.2 2.9 copy.102
  777.1 50.6 %all-gather.5.cloned.1.call-done = f32[768,768]{1,0:T(8,128)} async-done(((f32[96,768]{1,0:T(8,128)}), f32[768,768]{1,0:T(8,128)}) %all-gather.5.cloned.1.call-update) | async-done | bytes 2359312 | tf_op jit(solution)/shard_map/all_gather | solution.py:276
  827.7 3.2 copy.180
  (227 shorter events, 41.2 us)
Async XLA Ops:
  7.2 263.3 %copy-start = (bf16[1536,768]{1,0:T(8,128)(2,1)S(1)}, bf16[1536,768]{1,0:T(8,128)(2,1)}, u32[]{:S(2)}) copy-start(bf16[1536,768]{1,0:T(8,128)(2,1)} %param.22) | copy-start | bytes 7077892
  7.2 133.9 %all-reduce.6.cloned.1.call-start = ((), (), s32[]{:S(2)}) async-start(), calls=%async_computation.4 | async-start | bytes 9437184 | tf_op jit(solution)/shard_map/psum | solution.py:125
  11.2 2.1 copy-start.34
  11.2 2.7 copy-start.54
  25.5 3.6 copy-start.3
  25.6 7.1 copy-start.53
  34.4 5.7 copy-start.15
  34.5 6.7 copy-start.19
  44.2 217.1 %all-reduce.8.cloned.1.call-start = ((), (), s32[]{:S(2)}) async-start(), calls=%async_computation.5 | async-start | bytes 9437184 | tf_op jit(solution)/shard_map/psum | solution.py:132
  144.9 2.2 copy-start.2
  144.9 2.2 copy-start.39
  144.9 2.1 copy-start.32
  167.0 149.4 %all-reduce.10.cloned.1.call-start = ((), (), s32[]{:S(2)}) async-start(), calls=%async_computation.6 | async-start | bytes 1474560 | tf_op jit(solution)/shard_map/psum | solution.py:176
  172.6 9.3 %copy-start.26 = (bf16[3,80,192]{1,2,0:T(8,128)(2,1)}, bf16[3,80,192]{1,2,0:T(8,128)(2,1)S(1)}, u32[]{:S(2)}) copy-start(bf16[3,80,192]{1,2,0:T(8,128)(2,1)S(1)} %fusion.35) | copy-start | bytes 276484
  175.7 5.7 copy-start.10
  175.7 6.2 copy-start.8
  175.7 6.2 copy-start.48
  180.3 81.0 %copy-start.33 = (f32[1536]{0:T(1024)S(1)}, f32[1536]{0:T(1024)}, u32[]{:S(2)}) copy-start(f32[1536]{0:T(1024)} %copy-done.32) | copy-start | bytes 18436
  180.3 81.0 %copy-start.37 = (f32[1536]{0:T(1024)S(1)}, f32[1536]{0:T(1024)}, u32[]{:S(2)}) copy-start(f32[1536]{0:T(1024)} %copy-done.36) | copy-start | bytes 18436
  180.3 81.0 %copy-start.40 = (f32[768]{0:T(1024)S(1)}, f32[768]{0:T(1024)}, u32[]{:S(2)}) copy-start(f32[768]{0:T(1024)} %get-tuple-element.120) | copy-start | bytes 9220
  180.3 81.0 %copy-start.50 = (f32[768]{0:T(1024)S(1)}, f32[768]{0:T(1024)}, u32[]{:S(2)}) copy-start(f32[768]{0:T(1024)} %get-tuple-element.121) | copy-start | bytes 9220
  266.1 2.2 copy-start.4
  275.7 4.8 copy-start.17
  275.7 4.8 copy-start.9
  280.4 2.2 copy-start.22
  280.4 2.1 copy-start.6
  281.9 132.6 %reduce-scatter.5.cloned.1.call-start = ((), (), s32[]{:S(2)}) async-start(), calls=%async_computation.8 | async-start | bytes 2654208 | tf_op jit(solution)/shard_map/reduce_scatter | solution.py:252
  320.3 4.3 copy-start.11
  322.6 2.0 copy-start.16
  322.6 2.0 copy-start.31
  324.7 2.0 copy-start.12
  329.1 8.4 %copy-start.20 = (bf16[1536,1,192]{0,2,1:T(8,128)(2,1)}, bf16[1536,1,192]{0,2,1:T(8,128)(2,1)S(1)}, u32[]{:S(2)}) copy-start(bf16[1536,1,192]{0,2,1:T(8,128)(2,1)S(1)} %stack_reshape.17) | copy-start | bytes 1769476
  342.0 3.1 copy-start.23
  345.0 2.1 copy-start.18
  345.0 142.3 %reduce-scatter.9.cloned.1.call-start = ((), (), s32[]{:S(2)}) async-start(), calls=%async_computation.11 | async-start | bytes 2654208 | tf_op jit(solution)/shard_map/reduce_scatter | solution.py:252
  347.0 4.7 copy-start.14
  347.0 211.5 %reduce-scatter.11.cloned.1.call-start = ((), (), s32[]{:S(2)}) async-start(), calls=%async_computation.13 | async-start | bytes 2654208 | tf_op jit(solution)/shard_map/reduce_scatter | solution.py:252
  351.7 1.9 copy-start.21
  351.7 272.4 %reduce-scatter.7.cloned.1.call-start = ((), (), s32[]{:S(2)}) async-start(), calls=%async_computation.10 | async-start | bytes 884736 | tf_op jit(solution)/shard_map/reduce_scatter | solution.py:252
  353.3 366.4 %all-reduce.12.cloned.1.call-start = ((), (), s32[]{:S(2)}) async-start(), calls=%async_computation.7 | async-start | bytes 9437184 | tf_op jit(solution)/shard_map/psum | solution.py:224
  359.6 5.5 copy-start.38
  359.6 5.5 copy-start.41
  359.6 5.5 copy-start.7
  359.6 5.9 copy-start.49
  359.6 6.0 copy-start.52
  359.6 414.6 %all-gather.3.cloned.1.call-start = ((), (), s32[]{:S(2)}) async-start(), calls=%async_computation.9 | async-start | bytes 2654208 | tf_op jit(solution)/shard_map/all_gather | solution.py:274
  363.1 56.6 %copy-start.44 = (f32[768]{0:T(1024)S(1)}, f32[768]{0:T(1024)}, u32[]{:S(2)}) copy-start(f32[768]{0:T(1024)} %get-tuple-element.122) | copy-start | bytes 9220
  416.6 411.0 %all-gather.5.cloned.1.call-start = ((), (), s32[]{:S(2)}) async-start(), calls=%async_computation.12 | async-start | bytes 2654208 | tf_op jit(solution)/shard_map/all_gather | solution.py:276
  419.7 4.1 copy-start.45
  419.7 4.3 copy-start.47
  419.7 4.3 copy-start.46
  419.7 45.6 %copy-start.35 = (f32[6,768]{1,0:T(8,128)S(1)}, f32[6,768]{1,0:T(8,128)}, u32[]{:S(2)}) copy-start(f32[6,768]{1,0:T(8,128)} %param.33) | copy-start | bytes 55300
  419.7 46.9 %copy-start.42 = (f32[2,768]{1,0:T(2,128)S(1)}, f32[2,768]{1,0:T(2,128)}, u32[]{:S(2)}) copy-start(f32[2,768]{1,0:T(2,128)} %param.32) | copy-start | bytes 18436
  419.7 46.9 %copy-start.51 = (f32[2,2,768]{2,1,0:T(2,128)S(1)}, f32[2,2,768]{2,1,0:T(2,128)}, u32[]{:S(2)}) copy-start(f32[2,2,768]{2,1,0:T(2,128)} %param.39) | copy-start | bytes 36868
  419.7 48.1 %copy-start.43 = (f32[3072]{0:T(1024)S(1)}, f32[3072]{0:T(1024)}, u32[]{:S(2)}) copy-start(f32[3072]{0:T(1024)} %param.34) | copy-start | bytes 36868
  419.8 67.5 %copy-start.28 = (f32[2,96,768]{2,1,0:T(8,128)S(1)}, f32[2,96,768]{2,1,0:T(8,128)}, u32[]{:S(2)}) copy-start(f32[2,96,768]{2,1,0:T(8,128)} %param.37) | copy-start | bytes 1769476
  423.8 134.8 %copy-start.29 = (f32[2,96,768]{2,1,0:T(8,128)S(1)}, f32[2,96,768]{2,1,0:T(8,128)}, u32[]{:S(2)}) copy-start(f32[2,96,768]{2,1,0:T(8,128)} %param.38) | copy-start | bytes 1769476
  489.3 134.9 %copy-start.30 = (f32[96,192]{1,0:T(8,128)S(1)}, f32[96,192]{1,0:T(8,128)}, u32[]{:S(2)}) copy-start(f32[96,192]{1,0:T(8,128)} %copy.109) | copy-start | bytes 221188
  559.8 7.7 collective-permute-start
  567.7 91.7 %collective-permute-start.1 = (f32[2,96,768]{2,1,0:T(8,128)S(1)}, f32[2,96,768]{2,1,0:T(8,128)}, u32[]{:S(2)}, u32[]{:S(2)}) collective-permute-start(f32[2,96,768]{2,1,0:T(8,128)S(1)} %get-tuple-element.106), channel_id=1, source_target_pairs={{0,8},{4,12},{8,0},{12,4},{16,24},{20,28},{24,16},{28,20},{1,9},{5... | collective-permute-start | bytes 1769480 | tf_op jit(solution)/shard_map/ppermute | solution.py:27
  660.6 68.2 %collective-permute-start.2 = (f32[4,96,768]{2,1,0:T(8,128)S(1)}, f32[4,96,768]{2,1,0:T(8,128)S(1)}, u32[]{:S(2)}, u32[]{:S(2)}) collective-permute-start(f32[4,96,768]{2,1,0:T(8,128)S(1)} %bitcast.220), channel_id=1, source_target_pairs={{0,16},{4,20},{8,24},{12,28},{16,0},{20,4},{24,8},{28,12},{1,17},{... | collective-permute-start | bytes 3538952 | tf_op jit(solution)/shard_map/ppermute | solution.py:27
  719.6 6.6 copy-start.24
  719.6 6.6 copy-start.25
  729.0 101.9 %copy-start.1 = (bf16[1536,768]{1,0:T(8,128)(2,1)S(1)}, bf16[1536,768]{1,0:T(8,128)(2,1)}, u32[]{:S(2)}) copy-start(bf16[1536,768]{1,0:T(8,128)(2,1)} %param.22) | copy-start | bytes 7077892
  (4 other events, 4.0 us)
Sparse Core Ops, SparseCore 0:
  44.4 96.7 all-reduce.5
  167.1 94.1 all-reduce.7
  282.0 34.3 all-reduce.9
  345.1 69.3 reduce-scatter.4
  418.4 68.8 reduce-scatter.8
  490.6 67.8 reduce-scatter.10
  562.4 61.6 reduce-scatter.6
  626.6 92.9 all-reduce.11
  722.1 52.0 all-gather.2
  777.0 50.5 all-gather.4
